TPU v7x, 512 devices: a whole 4x4x16 slice. The times are simulated.
512 devices in a mesh: pair: 2 (over core), dp: 16 (over x, z_lo), fsdp: 16 (over y, z_hi).
Axes of the slice: x: 4, y: 4, z: 16 (z_hi: 4, z_lo: 4; z = z_hi * 4 + z_lo), core: 2. Of those that a mesh axis runs over, the one named last changes fastest.
Arguments:
- features: bfloat16 [2, 320, 262144], P('pair', None, ('dp', 'fsdp')), may hold values from -6 to 6
- level_gain: float32 [64, 320], replicated, may hold values from 0.5 to 1.5
- levels: int32 [64], replicated, may hold values from 0 to 63
- w_in: bfloat16 [2, 1280, 320], P('pair', 'fsdp'), may hold values from -0.3125 to 0.3125
- w_down: bfloat16 [2, 1280, 320], P('pair', 'fsdp'), may hold values from -0.15625 to 0.15625
- w_rgb: float32 [2, 3, 320], P('pair'), may hold values from -0.3125 to 0.3125
- target: float32 [3, 262144], P(None, ('dp', 'fsdp')), may hold values from -6 to 6
- counts: int32 [262144], P(('dp', 'fsdp')), may hold values from 1 to 1024
Outputs:
- predictions: float32 [2, 3, 262144], P('pair', None, ('dp', 'fsdp'))
- grad_in: float32 [2, 1280, 320], P('pair', 'fsdp')
- grad_down: float32 [2, 1280, 320], P('pair', 'fsdp')
All inputs are finite; a program needn't handle non-finite values.
Results may differ from a plain program's by a relative error of at most 0.0022.
Values may be sent and summed in bfloat16 or wider, within the bound.
A program may use at most 64 MiB of HBM per device.

v0:
```python
import math
import jax
import jax.numpy as jnp
from jax import lax
from jax.sharding import PartitionSpec as P

IMG_PIX = 4096
EPS = 1e-06
DISTILL = 1.0


def from_partner(value, axis, apart):
    return lax.ppermute(value, axis, [(i, i ^ 1 << apart) for i in range(lax.axis_size(axis))])


def contract_rows(left, right):
    return lax.dot_general(
        left, right, (((1,), (1,)), ((), ())), preferred_element_type=jnp.float32
    )


def on_device(features, level_gain, levels, w_in, w_down, w_rgb, target, counts):
    x_local = features[0]
    pixels = x_local.shape[1]
    offset = lax.axis_index(("dp", "fsdp")) * pixels
    image = offset // IMG_PIX
    level = jnp.sum(jnp.where(jnp.arange(levels.shape[0], dtype=jnp.int32) == image, levels, 0))
    table_rows = jnp.arange(level_gain.shape[0], dtype=jnp.int32)[:, None]
    gain = jnp.sum(jnp.where(table_rows == level, level_gain, 0.0), axis=0)
    xf = x_local.astype(jnp.float32)
    mean_sq = jnp.mean(xf * xf, axis=0, keepdims=True)
    normed = (xf * lax.rsqrt(mean_sq + EPS) * gain[:, None]).astype(jnp.bfloat16)
    high = lax.Precision.HIGHEST
    head_rows = lax.dot_general(
        w_down[0].astype(jnp.float32), w_rgb[0], (((1,), (1,)), ((), ())), precision=high
    )
    head = lax.all_gather(head_rows, "fsdp", axis=0, tiled=True)
    pre = jnp.dot(
        lax.all_gather(w_in[0], "fsdp", axis=0, tiled=True),
        normed,
        preferred_element_type=jnp.float32,
    )
    sig = jax.nn.sigmoid(pre)
    hidden = (pre * sig).astype(jnp.bfloat16)
    pred = jnp.dot(w_rgb[0], xf, precision=high) + jnp.dot(
        head.T, hidden.astype(jnp.float32), precision=high
    )
    partner = from_partner(pred, "pair", 0)
    pixels_all = pixels * lax.axis_size("dp") * lax.axis_size("fsdp")
    loss_scale = math.sqrt(xf.shape[0] / pixels_all)
    samples = counts.astype(jnp.float32)
    weight = samples / (samples + 64.0)
    g_pred = (weight * (pred - target) + DISTILL * (pred - partner)) * loss_scale
    g_hidden = jnp.dot(head, g_pred, precision=high)
    g_pre = (g_hidden * sig * (1.0 + pre * (1.0 - sig))).astype(jnp.bfloat16)
    channels = normed.shape[0]
    grad_head = lax.dot_general(
        hidden.astype(jnp.float32), g_pred, (((1,), (1,)), ((), ())), precision=high
    )
    partial_rows = lax.psum_scatter(
        jnp.concatenate([contract_rows(g_pre, normed), grad_head], axis=1),
        "fsdp",
        scatter_dimension=0,
        tiled=True,
    )
    totals = lax.psum(partial_rows, "dp")
    grad_down = jnp.dot(totals[:, channels:], w_rgb[0], precision=high)
    return (pred[None], totals[:, :channels][None], grad_down[None])


def solution(mesh):
    in_specs = (
        P("pair", None, ("dp", "fsdp")),
        P(),
        P(),
        P("pair", "fsdp", None),
        P("pair", "fsdp", None),
        P("pair", None, None),
        P(None, ("dp", "fsdp")),
        P(("dp", "fsdp")),
    )
    out_specs = (P("pair", None, ("dp", "fsdp")), P("pair", "fsdp", None), P("pair", "fsdp", None))
    return jax.shard_map(
        on_device, mesh=mesh, in_specs=in_specs, out_specs=out_specs, check_vma=False
    )
```

profile of v0, /device:TPU:2, one launch (start us, length us, event | category | flops | bytes accessed | tf_op | source)
XLA Modules:
  0.0 454.9 jit_solution(8733867722866475132)
XLA Ops:
  7.2 0.0 copy-start
  7.2 0.0 reduce-scatter.4.cloned.1.call-start
  7.2 0.8 copy-done
  8.0 0.8 convolution_bitcast_fusion.1
  8.8 58.8 %all-gather.1 = f32[16,80,3]{1,2,0:T(4,128)S(1)} all-gather(f32[1,80,3]{1,2,0:T(4,128)S(1)} %convolution_bitcast_fusion.1), channel_id=1, replica_groups=mesh['pair'=2,'dp'=16,'fsdp'=16] {'fsdp'}, dimensions={0}, use_global_device_ids=true | all-gather | bytes 16320 | tf_op jit(solution)/shard_map/all_gather | solution.py:37
  67.6 0.1 reshape.23
  67.7 74.1 %all-gather = bf16[1,1280,320]{2,1,0:T(8,128)(2,1)S(1)} all-gather(bf16[1,80,320]{2,1,0:T(8,128)(2,1)} %param.11), channel_id=2, replica_groups=mesh['pair'=2,'dp'=16,'fsdp'=16] {'fsdp'}, dimensions={1}, use_global_device_ids=true | all-gather | bytes 870400 | tf_op jit(solution)/shard_map/all_gather | solution.py:39
  141.8 1.3 fusion.24
  143.1 0.6 iota_compare_fusion
  143.8 1.2 fusion.7
  145.0 1.0 select_reduce_fusion
  146.0 3.2 fusion.3
  149.2 0.0 copy-start.1
  149.3 0.0 copy-start.2
  149.3 0.0 copy-start.4
  149.3 0.0 copy-start.3
  149.3 2.1 fusion.25
  151.4 0.0 copy-done.1
  151.4 0.0 copy-done.2
  151.4 0.4 convolution_add_fusion
  151.8 1.9 collective-permute-start
  153.7 0.0 copy-done.4
  153.8 1.1 collective-permute-done
  154.9 0.0 copy-done.3
  154.9 1.1 fusion.26
  156.0 5.7 %fusion.6 = bf16[1280,1024]{0,1:T(8,128)(2,1)S(1)} fusion(f32[1024,1280]{1,0:T(8,128)S(1)} %get-tuple-element.13, f32[1280,3]{0,1:T(4,128)S(1)} %reshape.23, f32[3,1024]{1,0:T(4,128)S(1)} %add_multiply_fusion), kind=kOutput, calls=%fused_computation.9 | convolution fusion | flops 58982400 | bytes 7891968 | tf_op jit(solution)/shard_map/dot_general | solution.py:54
  161.8 1.1 fusion.13
  162.8 0.1 pad_maximum_fusion
  163.0 1.8 copy.21
  164.8 0.0 reduce-scatter.4.cloned.1.call-update
  164.8 0.0 all-reduce.2.cloned.1.call-start
  164.8 121.5 %reduce-scatter.4.cloned.1.call-done = f32[80,323]{1,0:T(8,128)} async-done(((f32[1280,323]{1,0:T(8,128)}), f32[80,323]{1,0:T(8,128)}) %reduce-scatter.4.cloned.1.call-update) | async-done | bytes 103376
  286.3 1.7 copy.22
  288.0 0.0 all-reduce.2.cloned.1.call-update
  288.0 0.6 copy.18
  288.6 156.1 %all-reduce.2.cloned.1.call-done = f32[80,323]{0,1:T(8,128)} async-done(((f32[80,323]{0,1:T(8,128)}), f32[80,323]{0,1:T(8,128)}) %all-reduce.2.cloned.1.call-update) | async-done | bytes 103376 | tf_op jit(solution)/shard_map/psum | solution.py:66
  444.7 0.9 slice_bitcast_fusion
  445.6 0.8 copy.19
  446.4 1.7 convolution_bitcast_fusion
  (4 shorter events, 0.0 us)
Async XLA Ops:
  7.2 0.8 copy-start
  7.2 279.1 %reduce-scatter.4.cloned.1.call-start = ((), (), s32[]{:S(2)}) async-start(), calls=%async_computation.2 | async-start | bytes 2088960
  149.2 2.2 copy-start.1
  149.3 2.2 copy-start.2
  149.3 4.5 copy-start.4
  149.3 5.6 %copy-start.3 = (f32[3,1024]{1,0:T(4,128)S(1)}, f32[3,1024]{1,0:T(4,128)}, u32[]{:S(2)}) copy-start(f32[3,1024]{1,0:T(4,128)} %param.14) | copy-start | bytes 36868
  151.8 3.1 collective-permute-start
  164.8 279.9 %all-reduce.2.cloned.1.call-start = ((), (), s32[]{:S(2)}) async-start(), calls=%async_computation.1 | async-start | bytes 335872 | tf_op jit(solution)/shard_map/psum | solution.py:66
Sparse Core Ops, SparseCore 0:
  164.9 121.3 reduce-scatter.3
  289.5 155.1 all-reduce.1
where the time goes:
time: 455 us
  waiting for transfers between devices  279 us (61%)
  blocking collectives  133 us (29%)
  matrix products  16.1 us (4%)
  between operations  14.2 us (3%)
  local copies, waits for them, and re-layouts  6.68 us (1%)
    psum x1, waiting for transfers between devices, on_device(): totals = lax.psum(partial_rows, 'dp')  156 us
    unnamed x3, waiting for transfers between devices  122 us
    all_gather x1, blocking collectives, on_device(): lax.all_gather(w_in[0], 'fsdp', axis=0, tiled=True)  74.1 us
    all_gather x1, blocking collectives, on_device(): head = lax.all_gather(head_rows, 'fsdp', axis=0, tiled=True)  58.8 us
  transfers between devices with their start and end apart: 3, of which 3 were waited for; matrix products, arithmetic and copies ran while one was open for 0% of the time, Pallas kernels for 0%

commit v1 on v0

--- a/solution.py
+++ b/solution.py
@@ -63,7 +63,7 @@
         scatter_dimension=0,
         tiled=True,
     )
-    totals = lax.psum(partial_rows, "dp")
+    totals = jnp.sum(lax.all_gather(partial_rows, "dp"), axis=0)
     grad_down = jnp.dot(totals[:, channels:], w_rgb[0], precision=high)
     return (pred[None], totals[:, :channels][None], grad_down[None])
 

time: 455 us -> 386 us (0.85)
  the two profiles are of different devices: /device:TPU:2 before, /device:TPU:8 now
where the time goes in v1:
time: 386 us; the launch traced here: 385 us
  waiting for transfers between devices  220 us (57%)
  blocking collectives  124 us (32%)
  matrix products  15.4 us (4%)
  between operations  14.2 us (4%)
  other arithmetic  5.97 us (2%)
  local copies, waits for them, and re-layouts  3.96 us (1%)
    reduce_scatter x1, waiting for transfers between devices, on_device(): lax.psum_scatter(jnp.concatenate([contract_rows(g_pre, normed), grad_head...  129 us
    all_gather x1, waiting for transfers between devices, on_device(): totals = jnp.sum(lax.all_gather(partial_rows, 'dp'), axis=0)  89.4 us
    all_gather x1, blocking collectives, on_device(): lax.all_gather(w_in[0], 'fsdp', axis=0, tiled=True)  69.7 us
    all_gather x1, blocking collectives, on_device(): head = lax.all_gather(head_rows, 'fsdp', axis=0, tiled=True)  54.3 us
  transfers between devices with their start and end apart: 3, of which 3 were waited for; matrix products, arithmetic and copies ran while one was open for 0% of the time, Pallas kernels for 0%

profile of v1, /device:TPU:8, one launch (start us, length us, event | category | flops | bytes accessed | tf_op | source)
XLA Modules:
  0.0 385.2 jit_solution(464283421719356178)
XLA Ops:
  7.2 0.0 copy-start
  7.2 0.0 reduce-scatter.4.cloned.1.call-start
  7.2 0.8 copy-done
  8.0 0.8 convolution_bitcast_fusion.1
  8.8 54.3 %all-gather.2 = f32[16,80,3]{1,2,0:T(4,128)S(1)} all-gather(f32[1,80,3]{1,2,0:T(4,128)S(1)} %convolution_bitcast_fusion.1), channel_id=1, replica_groups=mesh['pair'=2,'dp'=16,'fsdp'=16] {'fsdp'}, dimensions={0}, use_global_device_ids=true | all-gather | bytes 16320 | tf_op jit(solution)/shard_map/all_gather | solution.py:37
  63.1 0.1 reshape.24
  63.2 69.7 %all-gather = bf16[1,1280,320]{2,1,0:T(8,128)(2,1)S(1)} all-gather(bf16[1,80,320]{2,1,0:T(8,128)(2,1)} %param.11), channel_id=2, replica_groups=mesh['pair'=2,'dp'=16,'fsdp'=16] {'fsdp'}, dimensions={1}, use_global_device_ids=true | all-gather | bytes 870400 | tf_op jit(solution)/shard_map/all_gather | solution.py:39
  132.9 1.3 fusion.24
  134.2 0.6 iota_compare_fusion
  134.9 1.2 fusion.7
  136.1 1.0 select_reduce_fusion
  137.1 3.2 fusion.3
  140.3 0.0 copy-start.1
  140.3 0.0 copy-start.2
  140.3 0.0 copy-start.4
  140.3 0.0 copy-start.3
  140.4 2.1 fusion.25
  142.5 0.0 copy-done.1
  142.5 0.0 copy-done.2
  142.5 0.4 convolution_add_fusion
  142.9 1.9 collective-permute-start
  144.8 0.0 copy-done.4
  144.8 1.1 collective-permute-done
  145.9 0.0 copy-done.3
  146.0 1.1 fusion.26
  147.1 5.7 %fusion.6 = bf16[1280,1024]{0,1:T(8,128)(2,1)S(1)} fusion(f32[1024,1280]{1,0:T(8,128)S(1)} %get-tuple-element.13, f32[1280,3]{0,1:T(4,128)S(1)} %reshape.24, f32[3,1024]{1,0:T(4,128)S(1)} %add_multiply_fusion), kind=kOutput, calls=%fused_computation.9 | convolution fusion | flops 58982400 | bytes 7891968 | tf_op jit(solution)/shard_map/dot_general | solution.py:54
  152.8 1.1 fusion.13
  153.9 0.1 pad_maximum_fusion
  154.0 1.8 copy.20
  155.8 0.0 reduce-scatter.4.cloned.1.call-update
  155.9 0.0 all-gather.5.cloned.1.call-start
  155.9 129.1 %reduce-scatter.4.cloned.1.call-done = f32[80,323]{1,0:T(8,128)} async-done(((f32[1280,323]{1,0:T(8,128)}), f32[80,323]{1,0:T(8,128)}) %reduce-scatter.4.cloned.1.call-update) | async-done | bytes 103376 | tf_op jit(solution)/shard_map/reduce_scatter | solution.py:60
  285.0 0.0 all-gather.5.cloned.1.call-update
  285.1 0.6 copy.18
  285.7 89.4 %all-gather.5.cloned.1.call-done = f32[1280,323]{1,0:T(8,128)} async-done(((f32[80,323]{1,0:T(8,128)}), f32[1280,323]{1,0:T(8,128)}) %all-gather.5.cloned.1.call-update) | async-done | bytes 1653776 | tf_op jit(solution)/shard_map/all_gather | solution.py:66
  375.0 1.7 reduce_sum.39
  376.7 0.7 slice_bitcast_fusion
  377.4 1.0 convolution_bitcast_fusion
  (4 shorter events, 0.0 us)
Async XLA Ops:
  7.2 0.8 copy-start
  7.2 277.9 %reduce-scatter.4.cloned.1.call-start = ((), (), s32[]{:S(2)}) async-start(), calls=%async_computation.2 | async-start | bytes 2088960 | tf_op jit(solution)/shard_map/reduce_scatter | solution.py:60
  140.3 2.2 copy-start.1
  140.3 2.2 copy-start.2
  140.3 4.5 %copy-start.4 = (s32[1024]{0:T(1024)S(1)}, s32[1024]{0:T(1024)}, u32[]{:S(2)}) copy-start(s32[1024]{0:T(1024)} %param.15) | copy-start | bytes 12292
  140.3 5.6 %copy-start.3 = (f32[3,1024]{1,0:T(4,128)S(1)}, f32[3,1024]{1,0:T(4,128)}, u32[]{:S(2)}) copy-start(f32[3,1024]{1,0:T(4,128)} %param.14) | copy-start | bytes 36868
  142.9 3.1 collective-permute-start
  155.9 219.2 %all-gather.5.cloned.1.call-start = ((), (), s32[]{:S(2)}) async-start(), calls=%async_computation.1 | async-start | bytes 2088960 | tf_op jit(solution)/shard_map/all_gather | solution.py:66
Sparse Core Ops, SparseCore 0:
  156.0 129.0 reduce-scatter.3
  287.3 87.6 all-gather.4

commit v2 on v0

--- a/solution.py
+++ b/solution.py
@@ -36,7 +36,9 @@
     )
     head = lax.all_gather(head_rows, "fsdp", axis=0, tiled=True)
     pre = jnp.dot(
-        lax.all_gather(w_in[0], "fsdp", axis=0, tiled=True),
+        jnp.concatenate(
+            lax.all_to_all(jnp.stack([w_in[0]] * lax.axis_size("fsdp")), "fsdp", 0, 0), axis=0
+        ),
         normed,
         preferred_element_type=jnp.float32,
     )

time: 455 us -> 420 us (0.923)
  blocking collectives: 133 us -> 87.6 us
  starting transfers between devices: 1.99 us -> 19.8 us
    all_gather x1 -> x0, blocking collectives: 74.1 us -> none  [on_device(): lax.all_gather(w_in[0], 'fsdp', axis=0, tiled=True)]
    all_gather x1, blocking collectives: 58.8 us -> 87.6 us  [on_device(): head = lax.all_gather(head_rows, 'fsdp', axis=0, tiled=True)]
    all_to_all x0 -> x1, starting transfers between devices: none -> 17.8 us  [on_device(): lax.all_to_all(jnp.stack([w_in[0]] * lax.axis_size('fsdp')), 'fsdp', 0, 0)]
  transfers between devices with their start and end apart: 3 -> 4, of which waited for: 3 -> 3; matrix products, arithmetic and copies ran while one was open for 0% -> 1% of each run, Pallas kernels for 0% -> 0%
where the time goes in v2:
time: 420 us
  waiting for transfers between devices  275 us (65%)
  blocking collectives  87.6 us (21%)
  starting transfers between devices  19.8 us (5%)
  matrix products  14.4 us (3%)
  between operations  14.2 us (3%)
  local copies, waits for them, and re-layouts  7.9 us (2%)
    psum x1, waiting for transfers between devices, on_device(): totals = lax.psum(partial_rows, 'dp')  156 us
    unnamed x3, waiting for transfers between devices  118 us
    all_gather x1, blocking collectives, on_device(): head = lax.all_gather(head_rows, 'fsdp', axis=0, tiled=True)  87.6 us
    all_to_all x1, starting transfers between devices, on_device(): lax.all_to_all(jnp.stack([w_in[0]] * lax.axis_size('fsdp')), 'fsdp', 0, 0)  17.8 us
  transfers between devices with their start and end apart: 4, of which 3 were waited for; matrix products, arithmetic and copies ran while one was open for 1% of the time, Pallas kernels for 0%

profile of v2, /device:TPU:2, one launch (start us, length us, event | category | flops | bytes accessed | tf_op | source)
XLA Modules:
  0.0 420.1 jit_solution(2379759073117273537)
XLA Ops:
  7.2 0.0 copy-start
  7.2 0.0 copy-start.3
  7.2 0.0 copy-start.6
  7.2 0.0 copy-start.2
  7.2 0.0 copy-start.1
  7.2 2.0 stack.3
  9.2 17.8 %all-to-all-start = ((bf16[16,80,320]{2,1,0:T(8,128)(2,1)}), bf16[16,80,320]{2,1,0:T(8,128)(2,1)S(1)}, u32[]{:S(2)}, u32[]{:S(2)}) async-start(bf16[16,80,320]{2,1,0:T(8,128)(2,1)} %stack.3), calls=%async_computation | async-start | bytes 1966080 | tf_op jit(solution)/shard_map/all_to_all | solution.py:40
  27.0 0.0 reduce-scatter.4.cloned.1.call-start
  27.1 0.0 copy-done
  27.1 0.0 copy-done.3
  27.1 0.1 convolution_bitcast_fusion.1
  27.2 87.6 %all-gather = f32[16,80,3]{1,2,0:T(4,128)S(1)} all-gather(f32[1,80,3]{1,2,0:T(4,128)S(1)} %convolution_bitcast_fusion.1), channel_id=1, replica_groups=mesh['pair'=2,'dp'=16,'fsdp'=16] {'fsdp'}, dimensions={0}, use_global_device_ids=true | all-gather | bytes 16320 | tf_op jit(solution)/shard_map/all_gather | solution.py:37
  114.8 0.1 reshape.39
  114.9 0.0 copy-done.6
  114.9 0.6 fusion.29
  115.6 0.6 iota_compare_fusion
  116.2 0.0 copy-done.2
  116.2 0.1 select_reduce_fusion
  116.3 0.0 copy-done.1
  116.3 0.2 fusion.7
  116.5 0.0 all-to-all-done
  116.5 2.1 fusion.3
  118.7 0.0 copy-start.5
  118.7 0.0 copy-start.4
  118.7 2.1 fusion.30
  120.8 0.4 convolution_add_fusion
  121.2 1.9 collective-permute-start
  123.1 0.0 copy-done.5
  123.1 1.1 collective-permute-done
  124.3 0.0 copy-done.4
  124.3 1.1 fusion.31
  125.4 5.7 %fusion.6 = bf16[1280,1024]{0,1:T(8,128)(2,1)S(1)} fusion(f32[1024,1280]{1,0:T(8,128)S(1)} %get-tuple-element.13, f32[1280,3]{0,1:T(4,128)S(1)} %reshape.39, f32[3,1024]{1,0:T(4,128)S(1)} %add_multiply_fusion), kind=kOutput, calls=%fused_computation.9 | convolution fusion | flops 58982400 | bytes 7891968 | tf_op jit(solution)/shard_map/dot_general | solution.py:56
  131.2 1.1 fusion.13
  132.2 0.1 pad_maximum_fusion
  132.4 1.8 copy.21
  134.2 0.0 reduce-scatter.4.cloned.1.call-update
  134.2 0.0 all-reduce.2.cloned.1.call-start
  134.3 117.5 %reduce-scatter.4.cloned.1.call-done = f32[80,323]{1,0:T(8,128)} async-done(((f32[1280,323]{1,0:T(8,128)}), f32[80,323]{1,0:T(8,128)}) %reduce-scatter.4.cloned.1.call-update) | async-done | bytes 103376
  251.7 1.7 copy.22
  253.4 0.0 all-reduce.2.cloned.1.call-update
  253.4 0.6 copy.18
  254.1 155.9 %all-reduce.2.cloned.1.call-done = f32[80,323]{0,1:T(8,128)} async-done(((f32[80,323]{0,1:T(8,128)}), f32[80,323]{0,1:T(8,128)}) %all-reduce.2.cloned.1.call-update) | async-done | bytes 103376 | tf_op jit(solution)/shard_map/psum | solution.py:68
  409.9 0.9 slice_bitcast_fusion
  410.9 0.8 copy.19
  411.6 1.7 convolution_bitcast_fusion
  (4 shorter events, 0.0 us)
Async XLA Ops:
  7.2 19.9 %copy-start = (bf16[1,80,320]{2,1,0:T(8,128)(2,1)S(1)}, bf16[1,80,320]{2,1,0:T(8,128)(2,1)}, u32[]{:S(2)}) copy-start(bf16[1,80,320]{2,1,0:T(8,128)(2,1)} %param.12) | copy-start | bytes 153604
  7.2 19.9 %copy-start.3 = (f32[1,3,320]{2,0,1:T(1,128)S(1)}, f32[1,3,320]{2,0,1:T(1,128)}, u32[]{:S(2)}) copy-start(f32[1,3,320]{2,0,1:T(1,128)} %param.13) | copy-start | bytes 11524
  7.2 107.7 %copy-start.6 = (s32[64]{0:T(128)S(1)}, s32[64]{0:T(128)}, u32[]{:S(2)}) copy-start(s32[64]{0:T(128)} %param.10) | copy-start | bytes 772
  7.2 109.0 %copy-start.2 = (f32[64,320]{1,0:T(8,128)S(1)}, f32[64,320]{1,0:T(8,128)}, u32[]{:S(2)}) copy-start(f32[64,320]{1,0:T(8,128)} %param.9) | copy-start | bytes 245764
  7.2 109.1 %copy-start.1 = (bf16[1,320,1024]{2,1,0:T(8,128)(2,1)S(1)}, bf16[1,320,1024]{2,1,0:T(8,128)(2,1)}, u32[]{:S(2)}) copy-start(bf16[1,320,1024]{2,1,0:T(8,128)(2,1)} %param.8) | copy-start | bytes 1966084
  9.2 107.3 %all-to-all-start = ((bf16[16,80,320]{2,1,0:T(8,128)(2,1)}), bf16[16,80,320]{2,1,0:T(8,128)(2,1)S(1)}, u32[]{:S(2)}, u32[]{:S(2)}) async-start(bf16[16,80,320]{2,1,0:T(8,128)(2,1)} %stack.3), calls=%async_computation | async-start | bytes 1966080 | tf_op jit(solution)/shard_map/all_to_all | solution.py:40
  27.0 224.7 %reduce-scatter.4.cloned.1.call-start = ((), (), s32[]{:S(2)}) async-start(), calls=%async_computation.3 | async-start | bytes 2088960
  118.7 4.5 %copy-start.5 = (s32[1024]{0:T(1024)S(1)}, s32[1024]{0:T(1024)}, u32[]{:S(2)}) copy-start(s32[1024]{0:T(1024)} %param.15) | copy-start | bytes 12292
  118.7 5.6 %copy-start.4 = (f32[3,1024]{1,0:T(4,128)S(1)}, f32[3,1024]{1,0:T(4,128)}, u32[]{:S(2)}) copy-start(f32[3,1024]{1,0:T(4,128)} %param.14) | copy-start | bytes 36868
  121.2 3.1 collective-permute-start
  134.2 275.7 %all-reduce.2.cloned.1.call-start = ((), (), s32[]{:S(2)}) async-start(), calls=%async_computation.2 | async-start | bytes 335872 | tf_op jit(solution)/shard_map/psum | solution.py:68
Sparse Core Ops, SparseCore 0:
  134.3 117.3 reduce-scatter.3
  254.9 154.9 all-reduce.1
